TPU v7x, 512 devices: a whole 4x8x8 slice. The times are simulated.
512 devices in a mesh: inner: 16 (over x_lo, z), outer: 32 (over x_hi, y, core).
Axes of the slice: x: 4 (x_hi: 2, x_lo: 2; x = x_hi * 2 + x_lo), y: 8, z: 8, core: 2. Of those that a mesh axis runs over, the one named last changes fastest.
Arguments:
- queries: float32 [65536, 1024], P(('outer', 'inner')), may hold values from -150 to 150, as said below
- keys: float32 [65536, 128], P(('outer', 'inner')), may hold values from -5 to 5
- values: float32 [65536, 128], P(('outer', 'inner')), may hold values from -6 to 6
- segment: int32 [65536], P(('outer', 'inner')), may hold values from 0 to 255, never falling along the last dimension, each value on 1 to 2048 neighbouring positions
Outputs:
- attended: float32 [65536, 1024], P(('outer', 'inner'))
Inputs may be any that keep to these rules, and one draw needn't show every extreme that they name: queries of a few tokens may be large multiples of earlier keys. `segment`: a trajectory holds at most 2048 tokens.
All inputs are finite; a program needn't handle non-finite values.
Results may differ from a plain program's by a relative error of at most 0.0003.
Values sent between devices are 32-bit elements; how exact they have to be, the bound alone decides.
A program may use at most 64 MiB of HBM per device.

v0:
```python
import functools
import math

import jax
import jax.numpy as jnp
from jax import lax
from jax.experimental import pallas as pl
from jax.experimental.pallas import tpu as pltpu
from jax.sharding import PartitionSpec as P

MESH = pl.DeviceIdType.MESH
F32, BF16 = jnp.float32, jnp.bfloat16

TOK = 128
HEADS = 8
SLOTS = 16
RING = 8
KEY_ROWS = TOK + 8
ROWS = KEY_ROWS + TOK
PARTS = ((0, KEY_ROWS), (KEY_ROWS, TOK))
MASKED = -1e30

ROUTES = (
    (1138688, 32580615, 77625346, 78672899, 5271556, 344070),
    (326435840, 9754632, 10501442, 338704693, 11849741, 1032204),
    (93390096, 77619266, 78675011, 72382532, 12612678, 475143),
    (9897985, 8707120, 325069251, 14691343, 272643381, 835596),
    (94439697, 78712064, 12652569, 32576520, 74479686, 475149),
    (10947586, 272639025, 8437771, 15741239, 273692982, 835597),
    (95489298, 79761665, 13702170, 268507145, 14711879, 475144),
    (11997187, 273688626, 9487372, 326156301, 14695686, 835592),
    (96538899, 80811266, 14751771, 74776586, 15802625, 475145),
    (13046788, 274738227, 10536973, 50381838, 15737095, 835593),
    (97588500, 81860867, 74776604, 336608267, 76810312, 475146),
    (14096389, 275787828, 11586574, 8439823, 9486385, 835594),
    (98638101, 74776852, 336622671, 337670216, 77859913, 475147),
    (15145990, 15742005, 8400948, 52438067, 11584522, 835584),
    (91543872, 324338783, 337672264, 30483764, 29436227, 507979),
    (15367, 14688262, 13640709, 12587018, 2100235, 786433),
    (1056768, 15737863, 10487814, 11537413, 13643780, 868366),
    (872227848, 871180528, 869326017, 203479883, 204527420, 245812),
    (77357057, 77596672, 78646279, 5320710, 81793101, 999439),
    (253700105, 1019018296, 870516784, 869469239, 56373302, 49156),
    (78406658, 3147528, 4194379, 80747596, 5249102, 999503),
    (254749706, 52179001, 871424195, 870318084, 57422903, 49157),
    (79456259, 4197129, 5243980, 7419981, 6373128, 999424),
    (255799307, 53228602, 1107140, 871424005, 6348558, 49152),
    (80505860, 5246730, 6293581, 83697742, 8135680, 999425),
    (256848908, 54278203, 2156741, 58778630, 7537423, 49153),
    (81555461, 6296331, 7343182, 81736, 815793993, 999426),
    (257898509, 55327804, 3206342, 59776058, 202432704, 49154),
    (82605062, 6103836, 4275207, 1049417, 816843594, 999427),
    (258948110, 208720957, 201379900, 202434619, 8587321, 49155),
    (871178247, 870130783, 882907136, 868226049, 5057538, 1032195),
    (8641551, 56819726, 55772173, 54724620, 204482571, 9),
)


def split(x):
    high = x.astype(BF16)
    return high, (x - high.astype(F32)).astype(BF16)


def bits(word, low, count):
    return lax.rem(lax.div(word, jnp.int32(1 << low)), jnp.int32(1 << count))


def doubled(x):
    high, low = split(x)
    return jnp.concatenate(
        [jnp.concatenate([high, high], axis=1), jnp.concatenate([low, low], axis=1)], axis=0
    )


def attend(kv, slot, mask, first, q_ref, acc, top, total):
    keys = doubled(kv[slot, 0:TOK, :])
    values = doubled(kv[slot, KEY_ROWS:ROWS, :].T)
    mask = jnp.concatenate([mask, mask], axis=1)
    for pair in range(HEADS // 2):
        cols = slice(pair * 2 * TOK, (pair + 1) * 2 * TOK)
        both = jnp.dot(keys, q_ref[:, cols], preferred_element_type=F32)
        scores = jnp.where(mask, both[:TOK] + both[TOK:], MASKED)
        high = jnp.max(scores, axis=0, keepdims=True)
        if not first:
            old = top[0:1, cols]
            high = jnp.maximum(old, high)
            factor = jnp.exp2(old - high)
        weights = jnp.exp2(scores - high)
        added = jnp.sum(weights, axis=0, keepdims=True)
        both = jnp.dot(values, jnp.concatenate(split(weights), axis=0), preferred_element_type=F32)
        mixed = both[:TOK] + both[TOK:]
        top[0:1, cols] = high
        if first:
            total[0:1, cols] = added
            acc[:, cols] = mixed
        else:
            total[0:1, cols] = total[0:1, cols] * factor + added
            acc[:, cols] = acc[:, cols] * factor + mixed


def kernel(
    planes, queries, keys, values, segment, out, kv, q_raw, q_ref, acc, top, total,
    load_sem, send_sem, extra_sem, recv_sem,
):
    inner, outer = lax.axis_index("inner"), lax.axis_index("outer")
    x, z = lax.div(inner, RING), lax.rem(inner, RING)
    plane, core = lax.div(outer, 2), lax.rem(outer, 2)
    up, down, across = lax.rem(z + 1, RING), lax.rem(z + RING - 1, RING), 1 - x
    ahead, behind = lax.rem(plane + 1, planes), lax.rem(plane + planes - 1, planes)

    def at(to_plane, to_x, to_z, to_core):
        return {"inner": to_x * RING + to_z, "outer": to_plane * 2 + to_core}

    near = [(x, up), (x, down), (across, z)]
    barrier = pltpu.get_barrier_semaphore()

    def greet(device):
        pl.semaphore_signal(barrier, inc=1, device_id=device, device_id_type=MESH)

    for to_x, to_z in near:
        for to_core in (0, 1):
            greet(at(plane, to_x, to_z, to_core))
    greet(at(plane, x, z, 1 - core))

    @pl.when(core == 0)
    def _():
        greet(at(behind, x, z, 1))

    @pl.when((core == 0) & (x == 0))
    def _():
        greet(at(behind, 1, z, 1))

    own = SLOTS
    loads = [
        pltpu.make_async_copy(keys, kv.at[own, pl.ds(0, TOK)], load_sem.at[0]),
        pltpu.make_async_copy(values, kv.at[own, pl.ds(KEY_ROWS, TOK)], load_sem.at[1]),
        pltpu.make_async_copy(queries, q_raw, load_sem.at[2]),
    ]
    for load in loads:
        load.start()
    own_seg = segment[...].astype(F32)
    kv[own, TOK:KEY_ROWS, :] = jnp.broadcast_to(own_seg, (8, TOK))

    place = inner * 2 + core
    words = [jnp.int32(0)] * 6
    for row, packed in enumerate(ROUTES):
        words = [jnp.where(place == row, jnp.int32(p), w) for p, w in zip(packed, words)]

    def entry(step):
        third, rest = lax.div(step, 3), lax.rem(step, 3)
        word = words[0]
        for n in range(1, 6):
            word = jnp.where(third == n, words[n], word)
        word = jnp.where(
            rest == 0, word, jnp.where(rest == 1, lax.div(word, 1 << 10), lax.div(word, 1 << 20))
        )
        return lax.rem(word, 1 << 10)

    def piece(held, slot, part, device, sem):
        first, count = PARTS[part]
        return pltpu.make_async_remote_copy(
            src_ref=kv.at[held, pl.ds(first, count)],
            dst_ref=kv.at[slot, pl.ds(first, count)],
            send_sem=sem,
            recv_sem=recv_sem.at[slot, part],
            device_id=device,
            device_id_type=MESH,
        )

    def onward(route, held, slot, part, act):
        for way, (to_x, to_z) in enumerate(near):
            device = at(plane, to_x, to_z, bits(route, 5 + 2 * way, 1))

            @pl.when(bits(route, 4 + 2 * way, 1) == 1)
            def _():
                act(piece(held, slot, part, device, send_sem.at[way, held, part]))

    def own_extra(part, act):
        @pl.when(core == 0)
        def _():
            act(piece(own, inner, part, at(plane, x, z, 1), extra_sem.at[0, part]))

        @pl.when(core == 1)
        def _():
            act(piece(own, inner, part, at(ahead, x, z, 0), extra_sem.at[0, part]))

        @pl.when((core == 1) & (x == 1))
        def _():
            act(piece(own, inner, part, at(ahead, 0, z, 0), extra_sem.at[1, part]))

    def start(copy):
        copy.start()

    def finish(copy):
        copy.wait_send()

    own_route = entry(jnp.int32(SLOTS))
    pl.semaphore_wait(barrier, 7 + core * (1 + x))
    loads[0].wait()
    onward(own_route, own, inner, 0, start)
    own_extra(0, start)
    loads[1].wait()
    onward(own_route, own, inner, 1, start)
    own_extra(1, start)

    loads[2].wait()
    scale = math.log2(math.e) / math.sqrt(TOK)
    for head in range(HEADS):
        cols = slice(head * TOK, (head + 1) * TOK)
        q_high, q_low = split(q_raw[:, cols].T * scale)
        q_ref[0:TOK, cols] = q_high
        q_ref[TOK : 2 * TOK, cols] = q_low

    row = lax.broadcasted_iota(jnp.int32, (TOK, TOK), 0)
    col = lax.broadcasted_iota(jnp.int32, (TOK, TOK), 1)
    seg_all = jnp.broadcast_to(own_seg, (TOK, TOK))
    attend(kv, own, (seg_all.T == seg_all) & (row <= col), True, q_ref, acc, top, total)

    lead = own_seg[:, 0:1]

    def step(n, carry):
        route = entry(n)
        slot = bits(route, 0, 4)
        for part in (0, 1):
            piece(slot, slot, part, at(plane, x, up, core), send_sem.at[0, slot, part]).wait_recv()
            onward(route, slot, slot, part, start)
        seg = kv[slot, TOK : TOK + 1, :]
        shared = jnp.sum(jnp.where(seg == lead, 1.0, 0.0), axis=1, keepdims=True)
        begin = jnp.where(own_seg == lead, TOK - shared, float(TOK))
        attend(kv, slot, row.astype(F32) >= begin, False, q_ref, acc, top, total)
        return carry

    lax.fori_loop(0, SLOTS, step, 0)

    for head in range(HEADS):
        cols = slice(head * TOK, (head + 1) * TOK)
        out[:, cols] = (acc[:, cols] / total[0:1, cols]).T

    def drain(n, carry):
        route = entry(n)
        slot = bits(route, 0, 4)
        for part in (0, 1):
            onward(route, slot, slot, part, finish)
        return carry

    lax.fori_loop(0, SLOTS, drain, 0)
    for part in (0, 1):
        onward(own_route, own, inner, part, finish)
        own_extra(part, finish)


def body(queries, keys, values, segment):
    planes = lax.axis_size("outer") // 2
    return pl.pallas_call(
        functools.partial(kernel, planes),
        name="gather_and_attend",
        out_shape=jax.ShapeDtypeStruct(queries.shape, F32),
        in_specs=[pl.BlockSpec(memory_space=pl.ANY)] * 3 + [pl.BlockSpec(memory_space=pltpu.VMEM)],
        out_specs=pl.BlockSpec(memory_space=pltpu.VMEM),
        scratch_shapes=[
            pltpu.VMEM((SLOTS + 1, ROWS, TOK), F32),
            pltpu.VMEM((TOK, HEADS * TOK), F32),
            pltpu.VMEM((2 * TOK, HEADS * TOK), BF16),
            pltpu.VMEM((TOK, HEADS * TOK), F32),
            pltpu.VMEM((8, HEADS * TOK), F32),
            pltpu.VMEM((8, HEADS * TOK), F32),
            pltpu.SemaphoreType.DMA((3,)),
            pltpu.SemaphoreType.DMA((3, SLOTS + 1, 2)),
            pltpu.SemaphoreType.DMA((2, 2)),
            pltpu.SemaphoreType.DMA((SLOTS, 2)),
        ],
        compiler_params=pltpu.CompilerParams(
            collective_id=0, has_side_effects=True, vmem_limit_bytes=24 << 20
        ),
    )(queries, keys, values, segment.reshape(1, TOK))


def solution(mesh):
    return jax.shard_map(
        body,
        mesh=mesh,
        in_specs=(
            P(("outer", "inner"), None),
            P(("outer", "inner"), None),
            P(("outer", "inner"), None),
            P(("outer", "inner")),
        ),
        out_specs=P(("outer", "inner"), None),
        check_vma=False,
    )
```

profile of v0, /device:TPU:64, one launch (start us, length us, event | category | flops | bytes accessed | tf_op | source)
XLA Modules:
  0.0 49.9 jit_solution(7031241964338392591)
XLA Ops:
  0.0 0.0 copy-start.3
  0.0 0.7 %copy-done.3 = s32[128]{0:T(128)S(1)} copy-done((s32[128]{0:T(128)S(1)}, s32[128]{0:T(128)}, u32[]{:S(2)}) %copy-start.3) | copy-done | bytes 536
  0.7 0.0 copy-start
  0.7 1.0 %copy-done = f32[128,1024]{1,0:T(8,128)S(1)} copy-done((f32[128,1024]{1,0:T(8,128)S(1)}, f32[128,1024]{1,0:T(8,128)}, u32[]{:S(2)}) %copy-start) | copy-done | bytes 524312
  1.7 0.0 copy-start.1
  1.7 0.8 %copy-done.1 = f32[128,128]{1,0:T(8,128)S(1)} copy-done((f32[128,128]{1,0:T(8,128)S(1)}, f32[128,128]{1,0:T(8,128)}, u32[]{:S(2)}) %copy-start.1) | copy-done | bytes 65560
  2.5 0.0 copy-start.2
  2.5 0.8 %copy-done.2 = f32[128,128]{1,0:T(8,128)S(1)} copy-done((f32[128,128]{1,0:T(8,128)S(1)}, f32[128,128]{1,0:T(8,128)}, u32[]{:S(2)}) %copy-start.2) | copy-done | bytes 65560
  3.4 45.7 %gather_and_attend.1 = f32[128,1024]{1,0:T(8,128)S(1)} custom-call(f32[128,1024]{1,0:T(8,128)S(1)} %copy-done, f32[128,128]{1,0:T(8,128)S(1)} %copy-done.1, f32[128,128]{1,0:T(8,128)S(1)} %copy-done.2, s32[1,128]{1,0:T(1,128)S(1)} %bitcast.1), custom_call_target="tpu_custom_call" | custom-call | tf_op jit(solution)/shard_map/gather_and_attend/pallas_call | solution.py:254
  49.1 0.8 %copy.6 = f32[128,1024]{1,0:T(8,128)} copy(f32[128,1024]{1,0:T(8,128)S(1)} %gather_and_attend.1) | data formatting | bytes 1048576
Async XLA Ops:
  0.0 0.7 %copy-start.3 = (s32[128]{0:T(128)S(1)}, s32[128]{0:T(128)}, u32[]{:S(2)}) copy-start(s32[128]{0:T(128)} %param.7) | copy-start | bytes 1540
  0.7 1.0 %copy-start = (f32[128,1024]{1,0:T(8,128)S(1)}, f32[128,1024]{1,0:T(8,128)}, u32[]{:S(2)}) copy-start(f32[128,1024]{1,0:T(8,128)} %queries.1) | copy-start | bytes 1572868
  1.7 0.8 %copy-start.1 = (f32[128,128]{1,0:T(8,128)S(1)}, f32[128,128]{1,0:T(8,128)}, u32[]{:S(2)}) copy-start(f32[128,128]{1,0:T(8,128)} %keys.1) | copy-start | bytes 196612
  2.5 0.8 %copy-start.2 = (f32[128,128]{1,0:T(8,128)S(1)}, f32[128,128]{1,0:T(8,128)}, u32[]{:S(2)}) copy-start(f32[128,128]{1,0:T(8,128)} %values.1) | copy-start | bytes 196612
where the time goes:
time: 50.2 us; the launch traced here: 49.9 us
  Pallas kernels  45.7 us (91%)
  local copies, waits for them, and re-layouts  4.17 us (8%)
    pallas_call x1, Pallas kernels, body(): pl.pallas_call(functools.partial(kernel, planes), name='gather_and_attend...  45.7 us
    unnamed x9, local copies, waits for them, and re-layouts  4.17 us

commit v1 on v0

v1 whole, which is shorter than its diff:
```python
import functools
import math

import jax
import jax.numpy as jnp
from jax import lax
from jax.experimental import pallas as pl
from jax.experimental.pallas import tpu as pltpu
from jax.sharding import PartitionSpec as P

MESH = pl.DeviceIdType.MESH
F32, BF16 = jnp.float32, jnp.bfloat16

TOK = 128
HEADS = 8
RING = 8
SLOTS = 16
PASSING = SLOTS
OWN = SLOTS + RING
KEY_ROWS = TOK + 8
ROWS = KEY_ROWS + TOK
PARTS = ((0, KEY_ROWS), (KEY_ROWS, TOK))
UP_HOPS = (4, 3)
LAG = 12
MASKED = -1e30

PLAN = (
    (278710033, 696010752, 311828512, 924845751, 694591521, 7612418, 556834486, 312576143, 859028486, 70931494, 11680309, 558420003, 380811269, 4404261, 12619885, 44, 2589072, 12465914, 50389),
    (820993, 679217184, 712804424, 10098792, 711527465, 116407306, 676375331, 575679566, 45650030, 47199812, 12332, 0, 0, 0, 0, 0, 9990657, 15049718, 52555),
    (412124161, 925280018, 704645760, 825567266, 859462954, 728763528, 279977492, 860004387, 314202215, 150591492, 12827684, 40424454, 216314389, 47289390, 5133, 0, 3809425, 7293816, 24044),
    (9470977, 841066242, 808583178, 8552554, 79306531, 112726056, 16552615, 49296070, 576297004, 48829454, 13357, 0, 0, 0, 0, 0, 3187345, 13584312, 56918),
    (705694337, 825632866, 859220105, 671091945, 704679700, 314364235, 559569924, 594579592, 8181068, 13636908, 593534184, 382768662, 106961039, 14727215, 0, 0, 236065, 5737547, 61293),
    (135301122, 44270602, 842016515, 809512041, 843186283, 8617996, 46667399, 14455912, 543243815, 49911853, 14382, 0, 0, 0, 0, 0, 12139026, 7703556, 61293),
    (3836546, 894043171, 860521867, 71444907, 178398997, 244592676, 315228981, 560496709, 862033165, 315628055, 81827976, 42523655, 15768942, 47, 0, 0, 4895026, 7164105, 63464),
    (36703362, 876620962, 910296107, 810559649, 844116074, 43102217, 543293453, 8486957, 82321190, 115907624, 48143, 0, 0, 0, 0, 0, 10570531, 6347205, 65144),
    (37753475, 416110243, 449631874, 828446370, 282105473, 571617078, 246723590, 211851799, 863118606, 43301098, 604536839, 8469543, 41263, 0, 0, 0, 1387572, 10397373, 36720),
    (12619780, 46929027, 12424355, 14424258, 47417387, 202386214, 544253966, 9471086, 15771495, 67141679, 40968, 0, 0, 0, 0, 0, 2839492, 7465581, 33017),
    (38803076, 417159844, 450681475, 896539299, 283154572, 8183426, 316846592, 906010210, 146095617, 144944431, 111158817, 310420488, 0, 0, 0, 0, 12991813, 12519214, 35233),
    (13669381, 47978628, 13473956, 82582659, 846367788, 15740014, 49327298, 302090240, 8455178, 101721130, 42024, 0, 0, 0, 0, 0, 3957973, 195559, 38938),
    (829430405, 418092070, 805966647, 776386567, 214998816, 181681795, 538479983, 539853964, 180625417, 146311529, 10530152, 42, 0, 0, 0, 0, 7360086, 10228733, 43906),
    (812685318, 846337038, 13866030, 15990980, 49516589, 8466720, 46138499, 370183272, 9439243, 102802475, 43018, 0, 0, 0, 0, 0, 5070454, 1281039, 41627),
    (8127110, 906663975, 452597135, 907712321, 675554446, 277002754, 841328164, 310906061, 640857098, 46346538, 11307, 0, 0, 0, 0, 0, 1437799, 14166350, 48291),
    (15768583, 116654214, 269779110, 8524878, 173127969, 9516072, 47188100, 304124009, 3156044, 36808748, 44043, 0, 0, 0, 0, 0, 14747383, 2399621, 45996),
    (837393, 696010760, 42654752, 694159218, 2106401, 10493033, 36362771, 49323023, 44047219, 14683797, 48311334, 112776227, 38810629, 38359604, 46207021, 12, 7508352, 11789999, 50389),
    (270313225, 815833096, 370541199, 504146607, 615778958, 786729095, 684957483, 584194051, 372415020, 38934092, 4132, 0, 0, 0, 0, 0, 717193, 7175138, 17859),
    (34612225, 857843474, 679487490, 780183586, 695206675, 101501955, 37411851, 7884815, 4872299, 13422639, 37854774, 113252366, 559469614, 5280870, 46093, 0, 565905, 12877747, 54638),
    (403743753, 849839882, 816980226, 917741858, 134754959, 852147459, 686132448, 585243652, 373464621, 39983693, 5157, 0, 0, 0, 0, 0, 12069401, 8270031, 22228),
    (10488457, 44141225, 101713683, 11538227, 826941475, 4956203, 13422592, 33657495, 594588181, 5323783, 559953717, 40942629, 6871149, 48338958, 0, 0, 11737641, 16105544, 59095),
    (143697930, 817301673, 169248897, 272380779, 306032776, 273167592, 852624015, 168410404, 552122437, 41033061, 6182, 0, 0, 0, 0, 0, 13308570, 1002883, 26462),
    (3844746, 826942475, 45786211, 35719988, 827330572, 104902657, 861544481, 38810629, 47798888, 6839296, 81822518, 7355430, 41475182, 47, 0, 0, 12761402, 886036, 63462),
    (45100170, 473706666, 507293833, 137114793, 237110532, 373458733, 274217096, 308066408, 6423119, 375423535, 39943, 0, 0, 0, 0, 0, 2702507, 6194205, 30223),
    (12587659, 105666219, 861546540, 715133955, 828476429, 47850533, 861964354, 15311878, 107502593, 7439406, 40910647, 49914376, 32, 0, 0, 0, 5483595, 1993005, 3975),
    (145797132, 179704589, 145199917, 178526030, 307433262, 238566537, 136583209, 308479791, 7439522, 106504, 33063, 0, 0, 0, 0, 0, 15355324, 2554165, 1921),
    (13637260, 106715820, 862596141, 14686212, 783323927, 70301734, 681582391, 545295375, 2730023, 49283593, 100764520, 35169281, 0, 0, 0, 0, 7032156, 9414462, 6402),
    (146846733, 180754190, 146249518, 274862927, 239910059, 8530278, 137632810, 309339496, 203465891, 67143681, 294945, 0, 0, 0, 0, 0, 16473805, 3639908, 297),
    (14686861, 107656983, 683719479, 7345928, 784372751, 116432680, 682622980, 34088036, 915410539, 1084938, 2664545, 34, 0, 0, 0, 0, 9199213, 10159351, 10771),
    (821082126, 854988941, 147298541, 275911944, 240427180, 212870439, 112333097, 268603393, 137439521, 104103978, 34818, 0, 0, 0, 0, 0, 9203198, 1358197, 8970),
    (8135310, 847951887, 684768359, 795718, 848999462, 68162656, 39332492, 583012449, 38643714, 582060555, 35843, 0, 0, 0, 0, 0, 14088078, 11277577, 15140),
    (148945935, 182852872, 278371624, 311564493, 174392493, 268578826, 312837253, 302158956, 304098370, 104901764, 3107, 0, 0, 0, 0, 0, 14252271, 379414, 13490),
)


def split(x):
    high = x.astype(BF16)
    return high, (x - high.astype(F32)).astype(BF16)


def across_lanes(both, blocks):
    return [
        both[:, 2 * n * TOK : (2 * n + 1) * TOK] + both[:, (2 * n + 1) * TOK : 2 * (n + 1) * TOK]
        for n in range(blocks)
    ]


def attend(kv, slots, masks, first, q_ref, acc, top, total):
    keys, values = [], []
    for slot in slots:
        k_high, k_low = split(kv[slot, 0:TOK, :])
        keys += [jnp.concatenate([k_high, k_high], axis=1), jnp.concatenate([k_low, k_low], axis=1)]
        values.append(jnp.concatenate(split(kv[slot, KEY_ROWS:ROWS, :]), axis=1))
    keys, values = jnp.concatenate(keys, axis=0), jnp.concatenate(values, axis=0)
    both = lax.dot_general(
        q_ref[...], keys, (((1,), (1,)), ((), ())), preferred_element_type=F32
    )
    scores = [
        jnp.where(jnp.concatenate([mask] * HEADS, axis=0), score, MASKED)
        for mask, score in zip(masks, across_lanes(both, len(slots)))
    ]
    high = functools.reduce(jnp.maximum, scores)
    high = jnp.broadcast_to(jnp.max(high, axis=1, keepdims=True), high.shape)
    if not first:
        old = top[...]
        high = jnp.maximum(old, high)
        factor = jnp.exp2(old - high)
    top[...] = high
    weights = [jnp.exp2(score - high) for score in scores]
    added = functools.reduce(jnp.add, weights)
    w_high, w_low = zip(*[split(weight) for weight in weights])
    both = jnp.dot(jnp.concatenate(w_high, axis=1), values, preferred_element_type=F32)
    rest = jnp.dot(jnp.concatenate(w_low, axis=1), values[:, :TOK], preferred_element_type=F32)
    mixed = across_lanes(both, 1)[0] + rest
    total[...] = added if first else total[...] * factor + added
    acc[...] = mixed if first else acc[...] * factor + mixed


def kernel(
    planes, queries, keys, values, segment, out, kv, q_raw, q_ref, acc, top, total,
    load_sem, send_sem, recv_sem,
):
    inner, outer = lax.axis_index("inner"), lax.axis_index("outer")
    x, z = lax.div(inner, RING), lax.rem(inner, RING)
    plane, core = lax.div(outer, 2), lax.rem(outer, 2)
    up, down, across = lax.rem(z + 1, RING), lax.rem(z + RING - 1, RING), 1 - x
    ahead, behind = lax.rem(plane + 1, planes), lax.rem(plane + planes - 1, planes)

    def at(to_plane, to_x, to_z, to_core):
        return {"inner": to_x * RING + to_z, "outer": to_plane * 2 + to_core}

    barrier = pltpu.get_barrier_semaphore()

    def greet(device):
        pl.semaphore_signal(barrier, inc=1, device_id=device, device_id_type=MESH)

    for to_x, to_z in ((x, up), (x, down), (across, z)):
        for to_core in (0, 1):
            greet(at(plane, to_x, to_z, to_core))
    greet(at(plane, x, z, 1 - core))

    @pl.when(core == 0)
    def _():
        greet(at(behind, x, z, 0))
        greet(at(behind, x, z, 1))

    @pl.when((core == 0) & (x == 0))
    def _():
        greet(at(behind, 1, z, 1))

    loads = [
        pltpu.make_async_copy(keys, kv.at[OWN, pl.ds(0, TOK)], load_sem.at[0]),
        pltpu.make_async_copy(values, kv.at[OWN, pl.ds(KEY_ROWS, TOK)], load_sem.at[1]),
        pltpu.make_async_copy(queries, q_raw, load_sem.at[2]),
    ]
    for load in loads:
        load.start()
    own_seg = segment[...].astype(F32)
    kv[OWN, TOK:KEY_ROWS, :] = jnp.broadcast_to(own_seg, (8, TOK))

    place = inner * 2 + core
    words = [jnp.int32(0)] * 19
    for row, packed in enumerate(PLAN):
        words = [jnp.where(place == row, jnp.int32(p), w) for p, w in zip(packed, words)]

    def lookup(options, n, each, width):
        word, rest = lax.div(n, each), lax.rem(n, each)
        packed = options[0]
        for k in range(1, len(options)):
            packed = jnp.where(word == k, options[k], packed)
        field = lax.rem(packed, 1 << width)
        for k in range(1, each):
            field = jnp.where(
                rest == k, lax.rem(lax.div(packed, 1 << (width * k)), 1 << width), field
            )
        return field

    def event_of(n):
        return lookup(words[:16], n, 3, 10)

    def slot_of(n):
        return lookup(words[16:], n, 6, 4)

    def bit(event, place):
        return lax.rem(lax.div(event, 1 << place), 2) == 1

    def piece(held, slot, part, device, way):
        first, count = PARTS[part]
        return pltpu.make_async_remote_copy(
            src_ref=kv.at[held, pl.ds(first, count)],
            dst_ref=kv.at[slot, pl.ds(first, count)],
            send_sem=send_sem.at[way, held, part],
            recv_sem=recv_sem.at[slot, part],
            device_id=device,
            device_id_type=MESH,
        )


    def onward(event, part, act):
        held = lax.rem(event, 32)
        index, passing = lax.rem(held, RING), held >= PASSING
        crossed = (held < PASSING) & (lax.div(held, RING) != x)
        is_o = passing | (~crossed & (core == 1) & (index < z))
        here = x * RING + index
        for way, to_z in ((0, up), (1, down)):
            below = index < to_z
            to_core = jnp.where(crossed, core, jnp.where(is_o == below, 1, 0))
            to_slot = jnp.where(is_o, jnp.where(below, here, PASSING + index), held)

            @pl.when(bit(event, 7 + way))
            def _():
                act(piece(held, to_slot, part, at(plane, x, to_z, to_core), way))

        @pl.when(bit(event, 9))
        def _():
            aside = {
                "inner": jnp.where(is_o, inner, across * RING + z),
                "outer": jnp.where(is_o, ahead * 2, plane * 2 + x),
            }
            act(piece(held, here, part, aside, 2))

    def own_onward(part, act):
        for way, to_z in ((0, up), (1, down)):
            hops = lax.rem(to_z - z + RING, RING)
            below = z < to_z
            to_core = jnp.where((core == 1) == below, 1, 0)
            to_slot = jnp.where((core == 1) & ~below, PASSING + z, inner)
            act(piece(OWN, to_slot, part, at(plane, x, to_z, to_core), way))

        @pl.when(core == 0)
        def _():
            act(piece(OWN, inner, part, at(plane, across, z, x), 2))
            act(piece(OWN, inner, part, at(plane, x, z, 1), 3))

        @pl.when(core == 1)
        def _():
            act(piece(OWN, inner, part, at(ahead, x, z, 0), 3))
            crossing = {
                "inner": across * RING + z,
                "outer": jnp.where(x == 0, plane * 2 + 1, ahead * 2),
            }
            act(piece(OWN, inner, part, crossing, 2))

    def start(copy):
        copy.start()

    def finish(copy):
        copy.wait_send()

    pl.semaphore_wait(barrier, 8 + core * x)
    for part in (0, 1):
        loads[part].wait()
        own_onward(part, start)

    loads[2].wait()
    scale = math.log2(math.e) / math.sqrt(TOK)
    for head in range(HEADS):
        rows = slice(head * TOK, (head + 1) * TOK)
        q_high, q_low = split(q_raw[:, rows] * scale)
        q_ref[rows, 0:TOK] = q_high
        q_ref[rows, TOK : 2 * TOK] = q_low

    row = lax.broadcasted_iota(jnp.int32, (TOK, TOK), 0)
    col = lax.broadcasted_iota(jnp.int32, (TOK, TOK), 1)
    seg_row = jnp.broadcast_to(own_seg, (TOK, TOK))
    seg_col = seg_row.T
    attend(kv, [OWN], [(seg_col == seg_row) & (col <= row)], True, q_ref, acc, top, total)

    lead = own_seg[:, 0:1]
    pieces = 2 * (SLOTS + (1 - core) * (RING - 1 - z))

    def pair(n):
        slots = [slot_of(2 * n), slot_of(2 * n + 1)]
        masks = []
        for slot in slots:
            seg = kv[slot, TOK : TOK + 1, :]
            shared = jnp.sum(jnp.where(seg == lead, 1.0, 0.0), axis=1, keepdims=True)
            masks.append((seg_col == lead) & (col.astype(F32) >= TOK - shared))
        attend(kv, slots, masks, False, q_ref, acc, top, total)

    def each_part(event, do):
        for part in (0, 1):

            @pl.when(bit(event, 5) == (part == 1))
            def _():
                do(part)

    def step(n, paired):
        event = event_of(n)

        def receive(part):
            slot = lax.rem(event, 32)
            piece(slot, slot, part, at(plane, x, up, core), 0).wait_recv()
            onward(event, part, start)

        each_part(event, receive)
        now = bit(event, 6)

        @pl.when(now)
        def _():
            pair(paired)

        @pl.when(n >= LAG)
        def _():
            drain(n - LAG, 0)

        return paired + jnp.where(now, 1, 0)

    def drain(n, carry):
        event = event_of(n)

        @pl.when(event >= 1 << 7)
        def _():
            each_part(event, lambda part: onward(event, part, finish))

        return carry

    paired = lax.fori_loop(0, pieces, step, jnp.int32(0))

    def rest(n, carry):
        pair(n)
        return carry

    lax.fori_loop(paired, SLOTS // 2, rest, 0)

    for head in range(HEADS):
        rows = slice(head * TOK, (head + 1) * TOK)
        out[:, rows] = acc[rows, :] / jnp.sum(total[rows, :], axis=1, keepdims=True)

    lax.fori_loop(pieces - LAG, pieces, drain, 0)
    for part in (0, 1):
        own_onward(part, finish)


def body(queries, keys, values, segment):
    planes = lax.axis_size("outer") // 2
    rows = HEADS * TOK
    return pl.pallas_call(
        functools.partial(kernel, planes),
        name="gather_and_attend",
        out_shape=jax.ShapeDtypeStruct(queries.shape, F32),
        in_specs=[pl.BlockSpec(memory_space=pltpu.HBM)] * 3 + [pl.BlockSpec(memory_space=pltpu.VMEM)],
        out_specs=pl.BlockSpec(memory_space=pltpu.VMEM),
        scratch_shapes=[
            pltpu.VMEM((OWN + 1, ROWS, TOK), F32),
            pltpu.VMEM((TOK, rows), F32),
            pltpu.VMEM((rows, 2 * TOK), BF16),
            pltpu.VMEM((rows, TOK), F32),
            pltpu.VMEM((rows, TOK), F32),
            pltpu.VMEM((rows, TOK), F32),
            pltpu.SemaphoreType.DMA((3,)),
            pltpu.SemaphoreType.DMA((4, OWN + 1, 2)),
            pltpu.SemaphoreType.DMA((OWN, 2)),
        ],
        compiler_params=pltpu.CompilerParams(
            collective_id=0, has_side_effects=True, vmem_limit_bytes=60 << 20
        ),
    )(queries, keys, values, segment.reshape(1, TOK))


def solution(mesh):
    return jax.shard_map(
        body,
        mesh=mesh,
        in_specs=(
            P(("outer", "inner"), None),
            P(("outer", "inner"), None),
            P(("outer", "inner"), None),
            P(("outer", "inner")),
        ),
        out_specs=P(("outer", "inner"), None),
        check_vma=False,
    )
```

time: 50.2 us -> 45.7 us (0.910)
  the two profiles are of different devices: /device:TPU:64 before, /device:TPU:6 now
where the time goes in v1:
time: 45.7 us; the launch traced here: 44.8 us
  Pallas kernels  42.9 us (94%)
  local copies, waits for them, and re-layouts  1.89 us (4%)
    pallas_call x1, Pallas kernels, body(): pl.pallas_call(functools.partial(kernel, planes), name='gather_and_attend...  42.9 us
    unnamed x1, local copies, waits for them, and re-layouts  1.89 us

profile of v1, /device:TPU:6, one launch (start us, length us, event | category | flops | bytes accessed | tf_op | source)
XLA Modules:
  0.0 44.8 jit_solution(3993118593408831609)
XLA Ops:
  0.0 42.9 %gather_and_attend.1 = f32[128,1024]{1,0:T(8,128)} custom-call(f32[128,1024]{1,0:T(8,128)} %queries.1, f32[128,128]{1,0:T(8,128)} %keys.1, f32[128,128]{1,0:T(8,128)} %values.1, s32[1,128]{1,0:T(1,128)} %bitcast.1), custom_call_target="tpu_custom_call" | custom-call | tf_op jit(solution)/shard_map/gather_and_attend/pallas_call | solution.py:325
  42.9 1.9 %copy.6 = f32[128,1024]{1,0:T(8,128)} copy(f32[128,1024]{1,0:T(8,128)} %gather_and_attend.1) | data formatting | bytes 1048576

commit v2 on v1

v2 whole, which is shorter than its diff:
```python
import functools
import math

import jax
import jax.numpy as jnp
from jax import lax
from jax.experimental import pallas as pl
from jax.experimental.pallas import tpu as pltpu
from jax.sharding import PartitionSpec as P

MESH = pl.DeviceIdType.MESH
F32, BF16 = jnp.float32, jnp.bfloat16

TOK = 128
HEADS = 8
RING = 8
SLOTS = 16
PASSING = SLOTS
OWN = SLOTS + RING
KEY_ROWS = TOK + 8
ROWS = KEY_ROWS + TOK
PARTS = ((0, KEY_ROWS), (KEY_ROWS, TOK))
UP_HOPS = (4, 3)
LAG = 12
MASKED = -1e30

PLAN = (
    (278710033, 34359296, 695607593, 35440641, 69918120, 694164746, 149981715, 728016935, 183507827, 11538069, 592481382, 5388852, 182997355, 47395877, 71348260, 12, 7504272, 15415034, 50389),
    (820993, 679217248, 9150242, 9478790, 710977027, 111164490, 14728995, 575745669, 112758830, 47779853, 12332, 0, 0, 0, 0, 0, 9990657, 15070118, 52555),
    (412124161, 925280018, 704645760, 825329930, 143445290, 558521347, 103981323, 8180407, 71981355, 13162639, 183603239, 314579509, 39991893, 47233061, 13317, 0, 9052305, 13584307, 54758),
    (807437313, 908108809, 44171274, 8618755, 12357255, 712090116, 678203499, 49295439, 575713894, 48829454, 13357, 0, 0, 0, 0, 0, 3187345, 7293816, 56924),
    (2786945, 825632866, 859220105, 671091945, 704679700, 314364235, 143152132, 105536780, 314745653, 594555973, 316168199, 660749349, 49289255, 14727270, 0, 0, 236065, 6146123, 59127),
    (135301122, 11275489, 9546531, 11577092, 167881856, 8467236, 46800389, 578589800, 16259149, 49395238, 47118, 0, 0, 0, 0, 0, 12165906, 7703616, 61398),
    (3836546, 826379905, 860521867, 211201162, 5002410, 105132201, 382523008, 282072608, 316168293, 561830024, 109066246, 7920678, 40910190, 47, 0, 0, 10137906, 9261252, 63462),
    (36833283, 136057058, 168832804, 810559595, 9449578, 134329125, 543175721, 8434784, 41958246, 644921863, 48143, 0, 0, 0, 0, 0, 11211811, 7145925, 63464),
    (707793539, 673993764, 449631692, 672143010, 145790285, 383289110, 179448630, 144202758, 40085774, 537713705, 8461614, 82878048, 41263, 0, 0, 0, 1387587, 15297213, 36720),
    (137400324, 844336901, 113379340, 170661899, 135375885, 115120138, 14713898, 48244295, 43007847, 100711424, 40968, 0, 0, 0, 0, 0, 11715892, 8264406, 33017),
    (38803076, 895891108, 862369411, 7102179, 40503566, 8182924, 537112878, 838966818, 146030145, 179448111, 44115489, 310386793, 0, 0, 0, 0, 15088965, 12519212, 35233),
    (138449925, 845386502, 114428941, 170930951, 48279566, 78777127, 35695695, 77642752, 75792385, 42042410, 41993, 0, 0, 0, 0, 0, 12834373, 994174, 38938),
    (39852677, 418143909, 451731076, 75141888, 108822669, 249171215, 385388033, 147621378, 180659273, 310521160, 44050978, 43, 0, 0, 0, 0, 7360086, 13180733, 47656),
    (139499526, 846436103, 115478542, 15742208, 49329316, 137376096, 46138376, 11640867, 76548449, 45196322, 43018, 0, 0, 0, 0, 0, 13952854, 1588239, 43922),
    (8002304, 710975264, 452724175, 710706885, 675494153, 539272366, 148476168, 11307304, 248818179, 45298211, 11372, 0, 0, 0, 0, 0, 5371504, 10650782, 48189),
    (268475399, 241467526, 139723791, 303046767, 48403470, 13737986, 43066500, 38045741, 3223626, 113282090, 44043, 0, 0, 0, 0, 0, 5371399, 4381070, 48186),
    (837393, 34359304, 924885655, 10148865, 2139169, 7350934, 35667475, 858823722, 6340278, 11537422, 48976934, 37344299, 81317893, 624997413, 71348260, 12, 10654080, 3925751, 50389),
    (270313225, 815898632, 687210785, 720798506, 686065986, 719461963, 3317611, 305273549, 241743404, 139498060, 4133, 0, 0, 0, 0, 0, 15769993, 13859810, 17862),
    (34612225, 858605609, 11149314, 44736546, 859655168, 78646304, 45634199, 104520711, 694162228, 12622863, 593607716, 39890950, 558971445, 5346350, 46093, 0, 688785, 13584187, 54758),
    (403743753, 849839882, 371335426, 917676811, 687082624, 720536076, 686666083, 306322436, 175683182, 140547661, 5158, 0, 0, 0, 0, 0, 12069401, 14992368, 22231),
    (714082953, 44140554, 102517761, 11538227, 826314376, 696427, 13422596, 558927968, 695211116, 594550581, 40932365, 47765583, 49289750, 48248934, 0, 0, 11737641, 7717896, 59133),
    (44180490, 135505282, 236727714, 818155307, 851807368, 550768872, 687116416, 5473069, 551851631, 40050222, 6183, 0, 0, 0, 0, 0, 3871386, 15783052, 26597),
    (715132554, 37364747, 69250836, 714919970, 4272129, 46171925, 5345928, 578828149, 559939685, 33600518, 39861110, 594655767, 40909831, 47, 0, 0, 1649466, 874572, 63462),
    (144747531, 885172611, 918693283, 177475714, 306317069, 919766242, 551818376, 853841000, 552605888, 653295910, 39943, 0, 0, 0, 0, 0, 4834219, 15043858, 32518),
    (12587659, 681611947, 70300437, 37399349, 13633541, 35690326, 6956077, 81790774, 34642473, 7887982, 16327479, 116957287, 32768, 0, 0, 0, 5483595, 14772690, 3975),
    (145797132, 180106628, 212645348, 138164485, 853906602, 274932899, 308821122, 854721641, 7374050, 109051912, 33063, 0, 0, 0, 0, 0, 5952700, 3118654, 1921),
    (13637260, 828413612, 4861037, 81826614, 40545286, 681621507, 863080215, 545261575, 82877994, 827439, 33655305, 34670121, 0, 0, 0, 0, 7032156, 9402942, 6402),
    (146846733, 181156229, 146651557, 139214150, 921873702, 8530148, 44309635, 309497192, 43124809, 101746689, 294912, 0, 0, 0, 0, 0, 11986381, 7572047, 297),
    (14686861, 829528749, 863645742, 8134661, 4209765, 40943276, 682623784, 613449828, 915975171, 36767242, 102279170, 34, 0, 0, 0, 0, 16539245, 10159239, 8611),
    (147896334, 182205830, 214810022, 275911944, 240427180, 76688679, 112501892, 239371265, 137373952, 111185184, 2082, 0, 0, 0, 0, 0, 9238238, 4307317, 10800),
    (16399112, 847951879, 684825647, 6357769, 39945001, 547358381, 35336197, 849350757, 548407916, 581994532, 35907, 0, 0, 0, 0, 0, 622478, 13259222, 15140),
    (276872207, 310779022, 278371502, 311564493, 174306561, 214205450, 46273792, 173320480, 11831362, 37792900, 3171, 0, 0, 0, 0, 0, 14253711, 5901334, 13490),
    (278710033, 695510802, 729598344, 694591754, 556940353, 251320618, 693143347, 33565696, 313735733, 36229122, 148093460, 41006087, 70299660, 106990598, 37786629, 4, 129673, 13098539, 17763),
    (820993, 9242656, 840999559, 110110375, 15739526, 111843843, 842020911, 116003851, 575247403, 47779917, 12332, 0, 0, 0, 0, 0, 9906177, 12468134, 52549),
    (446450057, 1704754, 772024353, 2403091, 103599767, 729305224, 313696523, 71094934, 13162639, 659590319, 4740396, 7387342, 104870957, 6329447, 5158, 0, 8560665, 14599163, 22132),
    (9470977, 841812009, 111280138, 9178272, 42765959, 45784075, 843717188, 49295439, 642822758, 115872782, 46093, 0, 0, 0, 0, 0, 3187345, 7293816, 56924),
    (413828737, 178015369, 858786282, 103568000, 381321483, 558894900, 142881431, 594579253, 4366700, 105404429, 593640749, 38845445, 74463278, 6331494, 0, 0, 11545233, 16599235, 26597),
    (135301122, 111313930, 43001603, 809512803, 843164800, 12656800, 42606085, 911776812, 15808006, 49395238, 47118, 0, 0, 0, 0, 0, 11770386, 5752836, 61398),
    (672828034, 706096916, 145609131, 827329673, 281192681, 928026240, 382238724, 282613796, 862303767, 14819333, 316708407, 106961000, 7355439, 39, 0, 0, 3840786, 15062208, 32616),
    (36703362, 809512098, 843252779, 44270602, 79701765, 911254572, 543293453, 8500256, 912275975, 644921384, 48143, 0, 0, 0, 0, 0, 10570531, 7144860, 63464),
    (828018307, 861287042, 828813986, 672412676, 146060388, 179930934, 145316869, 863118606, 178295849, 570949998, 106970118, 74522927, 40999, 0, 0, 0, 1920035, 959899, 34806),
    (137400324, 46928908, 12358883, 45881474, 10717197, 203200557, 544290858, 34650121, 82880359, 100711424, 40968, 0, 0, 0, 0, 0, 2839492, 7465581, 33017),
    (829067908, 674674061, 830115702, 283772933, 39640204, 6851072, 40155372, 284755744, 179616971, 9995466, 111191047, 310483976, 0, 0, 0, 0, 12735444, 1831022, 34729),
    (138449925, 47200006, 13473956, 879769731, 48279715, 136392551, 45088783, 49293410, 111443969, 42042376, 41993, 0, 0, 0, 0, 0, 12805333, 994174, 38938),
    (830117509, 863637902, 776387328, 284171040, 181613606, 538643759, 839982627, 146810370, 572892199, 213131436, 10595624, 42, 0, 0, 0, 0, 14025957, 2715967, 43916),
    (14718982, 116137093, 14523557, 268450948, 116559917, 8749068, 46271489, 104105000, 2106443, 35761193, 43018, 0, 0, 0, 0, 0, 5076454, 3247119, 41657),
    (711721606, 452411168, 777782917, 148905761, 41554185, 378714690, 344754724, 10663053, 312844803, 45714572, 11308, 0, 0, 0, 0, 0, 7429894, 9249950, 48186),
    (140549127, 49298688, 8749222, 81925377, 173311016, 9450606, 69248132, 12619885, 3221794, 36808748, 44043, 0, 0, 0, 0, 0, 1574647, 2415077, 45996),
    (837393, 695239442, 729597960, 34643969, 2840585, 727819795, 36490247, 693148682, 39849030, 592460842, 36814388, 72896526, 48245797, 37752939, 46183501, 12, 7508352, 15024038, 52555),
    (270313225, 815898632, 687210785, 787907370, 371865858, 719461899, 3317611, 305273549, 174699053, 38934092, 4132, 0, 0, 0, 0, 0, 15769993, 13859810, 17862),
    (824214529, 679480114, 713139209, 75810, 858827539, 3824736, 36707860, 859872951, 12277764, 13162502, 39955492, 16274997, 5353509, 48348174, 46093, 0, 665745, 13022323, 57077),
    (403743753, 849839882, 371335426, 917676811, 687082624, 720536076, 753709411, 585243652, 584228196, 39983693, 5157, 0, 0, 0, 0, 0, 12069401, 5161968, 22231),
    (714082953, 1058914, 101755667, 679481139, 780947491, 859832324, 695238667, 12626980, 46208533, 595383303, 627088485, 14211078, 15840294, 49330190, 0, 0, 8591913, 7719744, 65238),
    (143697930, 135505282, 236727714, 142872363, 176459532, 201593708, 687116813, 654095584, 585644037, 41098533, 6182, 0, 0, 0, 0, 0, 3871386, 16581832, 26462),
    (3844746, 893423241, 859835049, 4195426, 12594965, 861544481, 578858020, 559944812, 6394944, 34396695, 7354381, 661697574, 15841319, 47, 0, 0, 4270394, 6315147, 65149),
    (144747531, 818285802, 918981769, 177475714, 306317069, 919766242, 274217096, 135051368, 6831461, 586520608, 39943, 0, 0, 0, 0, 0, 4834219, 6196498, 32608),
    (716182155, 13390948, 715132554, 5288757, 828377187, 6395529, 14473250, 561055273, 14791718, 8182817, 612408366, 33555048, 48143, 0, 0, 0, 5491275, 14800530, 61575),
    (145797132, 180106628, 820884964, 178525322, 307433262, 274959497, 43125263, 854787366, 7439522, 109051912, 33063, 0, 0, 0, 0, 0, 15389884, 3107125, 1921),
    (717231756, 682727190, 6296374, 14330916, 39861079, 863643693, 545826819, 103856135, 2137609, 102761320, 68190761, 34716687, 0, 0, 0, 0, 14070876, 2651114, 7945),
    (146846733, 180754190, 146249518, 888279302, 239376555, 8530799, 137632810, 309339432, 43124963, 101746753, 294912, 0, 0, 0, 0, 0, 7036621, 3640052, 297),
    (718281357, 82598950, 862983820, 7387912, 41594981, 70440, 33657483, 848313865, 3779631, 37234753, 69773345, 34, 0, 0, 0, 0, 8150637, 12554312, 10771),
    (147896334, 182205830, 147701158, 343020808, 173318316, 212870503, 45393028, 370315265, 137439488, 111185184, 2082, 0, 0, 0, 0, 0, 9238238, 1358197, 10800),
    (8010504, 108706600, 814750349, 40674304, 15827629, 548024367, 38798405, 102541868, 548407300, 649103460, 35907, 0, 0, 0, 0, 0, 14063592, 1754608, 15140),
    (276872207, 310779022, 345414830, 311629965, 174306561, 147096586, 302191872, 312644716, 11831362, 37792900, 3171, 0, 0, 0, 0, 0, 14253711, 10862614, 13490),
)


def split(x):
    high = x.astype(BF16)
    return high, (x - high.astype(F32)).astype(BF16)


def across_lanes(both, blocks):
    return [
        both[:, 2 * n * TOK : (2 * n + 1) * TOK] + both[:, (2 * n + 1) * TOK : 2 * (n + 1) * TOK]
        for n in range(blocks)
    ]


def attend(kv, slots, masks, first, q_ref, acc, top, total):
    keys, values = [], []
    for slot in slots:
        k_high, k_low = split(kv[slot, 0:TOK, :])
        keys += [jnp.concatenate([k_high, k_high], axis=1), jnp.concatenate([k_low, k_low], axis=1)]
        values.append(jnp.concatenate(split(kv[slot, KEY_ROWS:ROWS, :]), axis=1))
    keys, values = jnp.concatenate(keys, axis=0), jnp.concatenate(values, axis=0)
    both = lax.dot_general(
        q_ref[...], keys, (((1,), (1,)), ((), ())), preferred_element_type=F32
    )
    scores = [
        jnp.where(jnp.concatenate([mask] * HEADS, axis=0), score, MASKED)
        for mask, score in zip(masks, across_lanes(both, len(slots)))
    ]
    high = functools.reduce(jnp.maximum, scores)
    high = jnp.broadcast_to(jnp.max(high, axis=1, keepdims=True), high.shape)
    if not first:
        old = top[...]
        high = jnp.maximum(old, high)
        factor = jnp.exp2(old - high)
    top[...] = high
    weights = [jnp.exp2(score - high) for score in scores]
    added = functools.reduce(jnp.add, weights)
    w_high, w_low = zip(*[split(weight) for weight in weights])
    both = jnp.dot(jnp.concatenate(w_high, axis=1), values, preferred_element_type=F32)
    rest = jnp.dot(jnp.concatenate(w_low, axis=1), values[:, :TOK], preferred_element_type=F32)
    mixed = across_lanes(both, 1)[0] + rest
    total[...] = added if first else total[...] * factor + added
    acc[...] = mixed if first else acc[...] * factor + mixed


def kernel(
    planes, queries, keys, values, segment, out, kv, seg_raw, q_raw, q_ref, acc, top, total,
    load_sem, send_sem, recv_sem,
):
    inner, outer = lax.axis_index("inner"), lax.axis_index("outer")
    x, z = lax.div(inner, RING), lax.rem(inner, RING)
    plane, core = lax.div(outer, 2), lax.rem(outer, 2)
    up, down, across = lax.rem(z + 1, RING), lax.rem(z + RING - 1, RING), 1 - x
    ahead, behind = lax.rem(plane + 1, planes), lax.rem(plane + planes - 1, planes)
    far = planes // 2
    last = plane == planes - 1

    def at(to_plane, to_x, to_z, to_core):
        return {"inner": to_x * RING + to_z, "outer": to_plane * 2 + to_core}

    loads = [
        pltpu.make_async_copy(segment, seg_raw, load_sem.at[0]),
        pltpu.make_async_copy(keys, kv.at[OWN, pl.ds(0, TOK)], load_sem.at[1]),
        pltpu.make_async_copy(values, kv.at[OWN, pl.ds(KEY_ROWS, TOK)], load_sem.at[2]),
        pltpu.make_async_copy(queries, q_raw, load_sem.at[3]),
    ]
    for load in loads:
        load.start()

    barrier = pltpu.get_barrier_semaphore()

    def greet(device):
        pl.semaphore_signal(barrier, inc=1, device_id=device, device_id_type=MESH)

    for to_x, to_z in ((x, up), (x, down), (across, z)):
        for to_core in (0, 1):
            greet(at(plane, to_x, to_z, to_core))
    greet(at(plane, x, z, 1 - core))

    @pl.when(core == 0)
    def _():
        greet(at(behind, x, z, 0))
        greet(at(behind, x, z, 1))

    @pl.when((core == 0) & (x == 0))
    def _():
        greet(at(behind, 1, z, 1))

    def lookup(options, n, each, width):
        word, rest = lax.div(n, each), lax.rem(n, each)
        packed = options[0]
        for k in range(1, len(options)):
            packed = jnp.where(word == k, options[k], packed)
        field = lax.rem(packed, 1 << width)
        for k in range(1, each):
            field = jnp.where(
                rest == k, lax.rem(lax.div(packed, 1 << (width * k)), 1 << width), field
            )
        return field

    def event_of(n):
        return lookup(words[:16], n, 3, 10)

    def slot_of(n):
        return lookup(words[16:], n, 6, 4)

    def bit(event, place):
        return lax.rem(lax.div(event, 1 << place), 2) == 1

    def piece(held, slot, part, device, way):
        first, count = PARTS[part]
        return pltpu.make_async_remote_copy(
            src_ref=kv.at[held, pl.ds(first, count)],
            dst_ref=kv.at[slot, pl.ds(first, count)],
            send_sem=send_sem.at[way, held, part],
            recv_sem=recv_sem.at[slot, part],
            device_id=device,
            device_id_type=MESH,
        )


    def absent(slot):
        kept = (lax.div(slot, RING) == x) & (lax.rem(slot, RING) < z)
        same = lax.div(slot, RING) == x
        return (plane == 0) & (core == 0) & (slot < PASSING) & ~kept & (same | (x == 0))

    def direct(index):
        return ~last & ((plane != far - 1) | ((x == 1) & (lax.rem(index, 2) == 0)))

    def onward(event, part, act):
        held = lax.rem(event, 32)
        index, passing = lax.rem(held, RING), held >= PASSING
        crossed = (held < PASSING) & (lax.div(held, RING) != x)
        is_o = passing | (~crossed & (core == 1) & (index < z))
        here = x * RING + index
        there = ~absent(held)
        for way, to_z in ((0, up), (1, down)):
            below = index < to_z
            to_core = jnp.where(crossed, core, jnp.where(is_o == below, 1, 0))
            to_slot = jnp.where(is_o, jnp.where(below, here, PASSING + index), held)

            @pl.when(bit(event, 7 + way) & there)
            def _():
                act(piece(held, to_slot, part, at(plane, x, to_z, to_core), way))

        @pl.when(bit(event, 9) & ~(is_o & ~direct(index)))
        def _():
            aside = {
                "inner": jnp.where(is_o, inner, across * RING + z),
                "outer": jnp.where(is_o, ahead * 2, plane * 2 + x),
            }
            act(piece(held, here, part, aside, 2))

        from_near = (plane == far - 1) & (x == 1) & (core == 1)
        from_far = (plane == far) & (x == 0) & (core == 0) & (lax.rem(index, 2) == 1)

        @pl.when(crossed & (index >= z) & (from_near | from_far))
        def _():
            aside = {
                "inner": jnp.where(from_near, z, RING + z),
                "outer": far * 2,
            }
            act(piece(held, held, part, aside, 2))

    def own_onward(part, act):
        for way, to_z in ((0, up), (1, down)):
            hops = lax.rem(to_z - z + RING, RING)
            below = z < to_z
            to_core = jnp.where((core == 1) == below, 1, 0)
            to_slot = jnp.where((core == 1) & ~below, PASSING + z, inner)
            act(piece(OWN, to_slot, part, at(plane, x, to_z, to_core), way))

        @pl.when(core == 0)
        def _():
            act(piece(OWN, inner, part, at(plane, across, z, x), 2))
            act(piece(OWN, inner, part, at(plane, x, z, 1), 3))

        @pl.when((core == 1) & direct(z))
        def _():
            act(piece(OWN, inner, part, at(ahead, x, z, 0), 3))

        @pl.when((core == 1) & ((x == 0) | ~last))
        def _():
            crossing = {
                "inner": across * RING + z,
                "outer": jnp.where(x == 0, plane * 2 + 1, ahead * 2),
            }
            act(piece(OWN, inner, part, crossing, 2))

    def start(copy):
        copy.start()

    def finish(copy):
        copy.wait_send()

    loads[0].wait()
    own_seg = seg_raw[...].astype(F32)
    kv[OWN, TOK:KEY_ROWS, :] = jnp.broadcast_to(own_seg, (8, TOK))
    pl.semaphore_wait(barrier, 8 + core * x)
    for part in (0, 1):
        loads[1 + part].wait()
        own_onward(part, start)

    place = inner * 2 + core + jnp.where(plane == far, 2 * SLOTS, 0)
    words = [jnp.int32(0)] * 19
    for row, packed in enumerate(PLAN):
        words = [jnp.where(place == row, jnp.int32(p), w) for p, w in zip(packed, words)]

    loads[3].wait()
    scale = math.log2(math.e) / math.sqrt(TOK)
    for head in range(HEADS):
        rows = slice(head * TOK, (head + 1) * TOK)
        q_high, q_low = split(q_raw[:, rows] * scale)
        q_ref[rows, 0:TOK] = q_high
        q_ref[rows, TOK : 2 * TOK] = q_low

    row = lax.broadcasted_iota(jnp.int32, (TOK, TOK), 0)
    col = lax.broadcasted_iota(jnp.int32, (TOK, TOK), 1)
    seg_row = jnp.broadcast_to(own_seg, (TOK, TOK))
    seg_col = seg_row.T
    attend(kv, [OWN], [(seg_col == seg_row) & (col <= row)], True, q_ref, acc, top, total)

    lead = own_seg[:, 0:1]
    pieces = 2 * (SLOTS + (1 - core) * (RING - 1 - z))

    def pair(n):
        slots = [slot_of(2 * n), slot_of(2 * n + 1)]
        masks = []
        for slot in slots:
            seg = kv[slot, TOK : TOK + 1, :]
            shared = jnp.sum(jnp.where(seg == lead, 1.0, 0.0), axis=1, keepdims=True)
            masks.append((seg_col == lead) & (col.astype(F32) >= TOK - shared))
        attend(kv, slots, masks, False, q_ref, acc, top, total)

    def each_part(event, do):
        for part in (0, 1):

            @pl.when(bit(event, 5) == (part == 1))
            def _():
                do(part)

    def step(n, paired):
        event = event_of(n)

        def receive(part):
            slot = lax.rem(event, 32)
            first, count = PARTS[part]

            @pl.when(absent(slot))
            def _():
                kv[slot, first : first + count, :] = jnp.zeros((count, TOK), F32)
                if part == 0:
                    kv[slot, TOK:KEY_ROWS, :] = jnp.full((8, TOK), -1.0, F32)

            @pl.when(~absent(slot))
            def _():
                piece(slot, slot, part, at(plane, x, up, core), 0).wait_recv()
                onward(event, part, start)

        each_part(event, receive)
        now = bit(event, 6)

        @pl.when(now)
        def _():
            pair(paired)

        @pl.when(n >= LAG)
        def _():
            drain(n - LAG, 0)

        return paired + jnp.where(now, 1, 0)

    def drain(n, carry):
        event = event_of(n)

        crosses = (plane == far - 1) | (plane == far)

        @pl.when((event >= 1 << 7) | crosses)
        def _():
            each_part(event, lambda part: onward(event, part, finish))

        return carry

    paired = lax.fori_loop(0, pieces, step, jnp.int32(0))

    def rest(n, carry):
        pair(n)
        return carry

    lax.fori_loop(paired, SLOTS // 2, rest, 0)

    for head in range(HEADS):
        rows = slice(head * TOK, (head + 1) * TOK)
        out[:, rows] = acc[rows, :] / jnp.sum(total[rows, :], axis=1, keepdims=True)

    lax.fori_loop(pieces - LAG, pieces, drain, 0)
    for part in (0, 1):
        own_onward(part, finish)


def body(queries, keys, values, segment):
    planes = lax.axis_size("outer") // 2
    rows = HEADS * TOK
    return pl.pallas_call(
        functools.partial(kernel, planes),
        name="gather_and_attend",
        out_shape=pltpu.VMEM(queries.shape, F32),
        in_specs=[pl.BlockSpec(memory_space=pltpu.HBM)] * 4,
        out_specs=pl.BlockSpec(memory_space=pltpu.VMEM),
        scratch_shapes=[
            pltpu.VMEM((OWN + 1, ROWS, TOK), F32),
            pltpu.VMEM((1, TOK), jnp.int32),
            pltpu.VMEM((TOK, rows), F32),
            pltpu.VMEM((rows, 2 * TOK), BF16),
            pltpu.VMEM((rows, TOK), F32),
            pltpu.VMEM((rows, TOK), F32),
            pltpu.VMEM((rows, TOK), F32),
            pltpu.SemaphoreType.DMA((4,)),
            pltpu.SemaphoreType.DMA((4, OWN + 1, 2)),
            pltpu.SemaphoreType.DMA((OWN, 2)),
        ],
        compiler_params=pltpu.CompilerParams(
            collective_id=0, has_side_effects=True, vmem_limit_bytes=60 << 20
        ),
    )(queries, keys, values, segment.reshape(1, TOK))


def solution(mesh):
    return jax.shard_map(
        body,
        mesh=mesh,
        in_specs=(
            P(("outer", "inner"), None),
            P(("outer", "inner"), None),
            P(("outer", "inner"), None),
            P(("outer", "inner")),
        ),
        out_specs=P(("outer", "inner"), None),
        check_vma=False,
    )
```

time: 45.7 us -> 42.4 us (0.928); the launches traced: 44.8 us -> 42.3 us
  Pallas kernels: 42.9 us -> 41.5 us
  local copies, waits for them, and re-layouts: 1.89 us -> 0.8 us
    pallas_call x1, Pallas kernels: 42.9 us -> 41.5 us  [body(): pl.pallas_call(functools.partial(kernel, planes), name='gather_and_attend...]
    unnamed x1, local copies, waits for them, and re-layouts: 1.89 us -> 0.8 us
where the time goes in v2:
time: 42.4 us; the launch traced here: 42.3 us
  Pallas kernels  41.5 us (98%)
  local copies, waits for them, and re-layouts  0.8 us (2%)
    pallas_call x1, Pallas kernels, body(): pl.pallas_call(functools.partial(kernel, planes), name='gather_and_attend...  41.5 us

profile of v2, /device:TPU:6, one launch (start us, length us, event | category | flops | bytes accessed | tf_op | source)
XLA Modules:
  0.0 42.3 jit_solution(8410853047020314602)
XLA Ops:
  0.0 41.5 %gather_and_attend.1 = f32[128,1024]{1,0:T(8,128)S(1)} custom-call(f32[128,1024]{1,0:T(8,128)} %queries.1, f32[128,128]{1,0:T(8,128)} %keys.1, f32[128,128]{1,0:T(8,128)} %values.1, s32[1,128]{1,0:T(1,128)} %bitcast.1), custom_call_target="tpu_custom_call" | custom-call | tf_op jit(solution)/shard_map/gather_and_attend/pallas_call | solution.py:396
  41.5 0.8 %copy.6 = f32[128,1024]{1,0:T(8,128)} copy(f32[128,1024]{1,0:T(8,128)S(1)} %gather_and_attend.1) | data formatting | bytes 1048576

commit v3 on v2

v3 whole, which is shorter than its diff:
```python
import functools
import math

import jax
import jax.numpy as jnp
from jax import lax
from jax.experimental import pallas as pl
from jax.experimental.pallas import tpu as pltpu
from jax.sharding import PartitionSpec as P

MESH = pl.DeviceIdType.MESH
F32, BF16 = jnp.float32, jnp.bfloat16

TOK = 128
HEADS = 8
RING = 8
SLOTS = 16
PASSING = SLOTS
OWN = SLOTS + RING
KEY_ROWS = TOK + 8
ROWS = KEY_ROWS + TOK
PARTS = ((0, KEY_ROWS), (KEY_ROWS, TOK))
UP_HOPS = (4, 3)
LAG = 12
MASKED = -1e30

PLAN = (
    (345014272, 311828481, 2596897, 217062666, 379624482, 39917743, 5388291, 249572387, 214996267, 4305956, 45068, 0, 0, 0, 0, 0, 7504272, 12465914, 50389),
    (840779521, 100664113, 695869186, 711992082, 42764983, 10099506, 43519638, 727722662, 49826831, 111971973, 693123891, 48796683, 45617781, 591476260, 46249556, 12, 9971457, 15049718, 52555),
    (412189697, 2818473, 346065568, 3285290, 280005864, 71609351, 12729383, 183507044, 148937068, 38844421, 13421, 0, 0, 0, 0, 0, 9052305, 13584307, 54758),
    (807502849, 43796489, 11389730, 44829824, 9194720, 678470435, 695217971, 779637316, 45801252, 745328655, 49960972, 15260262, 558936613, 609270325, 13357, 0, 3187345, 7320696, 54764),
    (705694401, 144058466, 3319210, 280006336, 313529056, 281223204, 176166188, 38870029, 41106733, 6405158, 14382, 0, 0, 0, 0, 0, 236065, 13995083, 59127),
    (135366658, 11275489, 842050323, 43001715, 826289924, 843251755, 12813108, 558899717, 46961704, 861560519, 661665319, 543725583, 594040941, 14727215, 0, 0, 12139026, 8148996, 61398),
    (3836610, 414909475, 4632225, 178398410, 671191308, 244323628, 282170912, 142612781, 316774414, 7380072, 48143, 0, 0, 0, 0, 0, 4895026, 7164060, 63374),
    (203459587, 827068578, 45220875, 236770084, 827337477, 844116010, 928034825, 543175721, 114841728, 8422182, 544291638, 48798824, 83418711, 47, 0, 0, 10570531, 448965, 65144),
    (37753475, 740700899, 73042348, 282105473, 6849675, 144944493, 283255846, 7864554, 570533166, 8469543, 41263, 0, 0, 0, 0, 0, 1387572, 10397373, 36720),
    (137465860, 171726597, 861705228, 811796524, 828540939, 845196365, 862061613, 544225354, 628130858, 116169737, 43073335, 116424704, 40968, 0, 0, 0, 11715892, 15145686, 36617),
    (38803076, 741750500, 774904237, 283154572, 537047682, 384337927, 906495015, 317926671, 571649162, 75540553, 303145, 0, 0, 0, 0, 0, 12991813, 12519394, 35233),
    (138515461, 14441222, 48011428, 812781430, 171727884, 46963726, 12442670, 81026, 116426795, 77595936, 8487978, 43032649, 0, 0, 0, 0, 7591493, 994284, 38938),
    (39852677, 742800101, 7781120, 148669156, 351931431, 317896193, 539788899, 277032969, 312051884, 77897867, 43051, 0, 0, 0, 0, 0, 7360086, 2888701, 43913),
    (139565062, 173825799, 862993191, 268636206, 171981837, 116438304, 1182732, 36745288, 78749985, 35660802, 10595433, 42, 0, 0, 0, 0, 321366, 8469757, 43922),
    (8002304, 778862631, 874124687, 907711919, 675494153, 182723074, 148219428, 540903720, 312718346, 46281315, 11307, 0, 0, 0, 0, 0, 1439239, 13797710, 48186),
    (268540935, 302005382, 269597862, 14753925, 109348005, 138425454, 43000834, 104903970, 3158090, 44150819, 44043, 0, 0, 0, 0, 0, 1439239, 5057000, 47811),
    (837457, 695238664, 729630760, 1886217, 694191145, 10487823, 727759879, 556836903, 6371362, 3823411, 78682158, 36744757, 557847565, 37852788, 113315885, 12, 8329600, 3894826, 50389),
    (9217865, 816120872, 303709568, 917159328, 141888142, 786729483, 918172839, 584060038, 583178595, 38934092, 4132, 0, 0, 0, 0, 0, 11469193, 4044770, 17862),
    (34677761, 858540137, 11149314, 44075688, 696011840, 71093280, 557878283, 16505899, 5033991, 116432534, 593530892, 46143502, 107501109, 47298597, 13317, 0, 665745, 12908467, 54758),
    (403809289, 849839882, 304226562, 918367400, 687082624, 720536076, 753709411, 585243652, 584228196, 38935117, 5158, 0, 0, 0, 0, 0, 12069401, 5161968, 22231),
    (10488521, 111184553, 102517761, 11538227, 826314376, 4956203, 12583732, 46235684, 5987861, 7921461, 15766541, 40941078, 107599919, 14727174, 0, 0, 11737641, 14008392, 59127),
    (143763466, 438543746, 168953611, 818155371, 851807368, 550768872, 687116416, 586384173, 307771461, 41033326, 6182, 0, 0, 0, 0, 0, 3871386, 15783052, 26597),
    (715132618, 37364747, 2207508, 781224756, 1052684, 35410988, 861544548, 38810629, 67656296, 861935661, 39860320, 594655767, 49323023, 7, 0, 0, 13183802, 886081, 32742),
    (211856395, 885394602, 851584419, 177475778, 135498509, 919766308, 274217096, 853841000, 6831296, 653295910, 39943, 0, 0, 0, 0, 0, 2737067, 15043860, 32518),
    (79696523, 827364011, 3811436, 715134773, 2176035, 47224598, 6326985, 1063734, 34708009, 7453207, 41427831, 578813967, 32879, 0, 0, 0, 5483595, 14772525, 3975),
    (145862668, 180106628, 212710820, 820160773, 853906563, 552740067, 43260034, 854721894, 7374050, 309436424, 32768, 0, 0, 0, 0, 0, 5952700, 3107134, 1921),
    (80746124, 828413612, 4861037, 14687030, 830123108, 115382275, 8005667, 16262007, 69246506, 546356224, 579963688, 34604128, 0, 0, 0, 0, 7032156, 9402942, 4242),
    (146912269, 181156229, 146651557, 341971727, 239376555, 8530799, 44309635, 309497192, 43124809, 67143681, 294945, 0, 0, 0, 0, 0, 7071181, 7572212, 297),
    (81795725, 40656557, 684514414, 8134661, 717329423, 847297575, 682623044, 613449828, 649070377, 547392515, 580913249, 34, 0, 0, 0, 0, 8150637, 12125327, 10771),
    (147961870, 181803791, 214810022, 275911944, 240427180, 212870439, 112501892, 268436644, 302351370, 111185027, 2082, 0, 0, 0, 0, 0, 9238238, 1358197, 10800),
    (8010504, 720150607, 684833831, 7087168, 40674336, 1054445, 750818826, 583012449, 38643714, 649103883, 35843, 0, 0, 0, 0, 0, 9500648, 11277782, 15140),
    (276937743, 310779022, 278371502, 311564493, 174392493, 10629376, 302126369, 312644716, 78940226, 37792900, 3171, 0, 0, 0, 0, 0, 14253711, 10862614, 13490),
    (311828809, 1321448, 305295, 100697327, 2108558, 7646382, 147949574, 46248998, 72364071, 105942019, 4132, 0, 0, 0, 0, 0, 129673, 8217278, 17724),
    (840779521, 100664113, 824189698, 695247495, 712804361, 857843383, 78273158, 540032678, 556842678, 676345962, 842683403, 859346030, 541175349, 558469133, 47763500, 12, 9906177, 6175478, 52555),
    (671589769, 278922912, 2467937, 176195720, 150252875, 36707331, 381860876, 48380007, 4240390, 107057165, 37893, 0, 0, 0, 0, 0, 8560905, 15191867, 22093),
    (9536513, 892078121, 11324194, 167880832, 825238275, 12356712, 541728563, 16274071, 843099815, 859845303, 694206086, 82352172, 48880165, 626578949, 13421, 0, 8430225, 13585267, 54758),
    (413828801, 177350122, 36306946, 381387019, 281157635, 381853731, 315634692, 116429007, 48241669, 40974373, 6182, 0, 0, 0, 0, 0, 11544993, 16047235, 26597),
    (135366658, 111313930, 826018825, 926714921, 827068427, 843251755, 859996172, 542154824, 844715052, 861560455, 14261263, 543743526, 47765551, 48249430, 0, 0, 11770386, 7718916, 60918),
    (672828098, 448147169, 143894666, 177483779, 381718144, 282071648, 15053860, 5283976, 49657893, 39917583, 7207, 0, 0, 0, 0, 0, 3779346, 5821452, 30462),
    (203459587, 809512098, 11358251, 859965220, 12747818, 10245957, 43881516, 201340725, 47733254, 9279520, 544291638, 628144168, 595106831, 47, 0, 0, 1723171, 6347100, 63464),
    (415928003, 707244674, 282071681, 315723915, 144879201, 178263310, 316810277, 638058601, 317724687, 42016806, 40007, 0, 0, 0, 0, 0, 1917635, 648619, 30831),
    (137465860, 46928908, 844271381, 137221131, 829167629, 47351851, 14691174, 44173110, 561035847, 101721895, 110182199, 100663343, 40968, 0, 0, 0, 2839492, 1567341, 33017),
    (416977604, 708294275, 283120780, 247502466, 640155950, 605847558, 146029606, 571649327, 9480394, 108076040, 303145, 0, 0, 0, 0, 0, 15487956, 1832450, 35194),
    (138515461, 828389126, 845320237, 137376566, 830282766, 48401452, 15740775, 112331639, 67143727, 1343498, 34646088, 43000936, 0, 0, 0, 0, 3957973, 195454, 38938),
    (418027205, 872856196, 148734628, 674511878, 181928998, 907578735, 9580551, 276864514, 312051948, 377531531, 43018, 0, 0, 0, 0, 0, 14025957, 2912575, 43193),
    (14784518, 830217349, 846369902, 15742775, 47448196, 369147044, 137437196, 109052972, 78939171, 2139209, 10520683, 42, 0, 0, 0, 0, 5076454, 1281039, 41657),
    (711787142, 676740960, 710328065, 278018913, 539627527, 277067815, 310748708, 540838029, 379827210, 46763148, 11307, 0, 0, 0, 0, 0, 7429894, 13797710, 48186),
    (140614663, 116654095, 75792550, 269620238, 173062184, 9516321, 138454018, 77631597, 3508236, 36808748, 44043, 0, 0, 0, 0, 0, 15206135, 2414869, 45996),
    (837457, 824214167, 1886903, 77223969, 556802050, 858791606, 693215273, 108038154, 44618758, 591477798, 49827843, 36711429, 4232270, 112244772, 46248973, 12, 7506192, 4538218, 52670),
    (9217865, 816055400, 303432335, 916882095, 304417422, 786967687, 752659623, 584060038, 241471020, 38934092, 4132, 0, 0, 0, 0, 0, 10547593, 4044770, 17862),
    (824214593, 2761522, 36347913, 892338281, 859462688, 44043274, 8052308, 37378868, 40898571, 104902198, 40391750, 38813237, 46251020, 48314373, 13357, 0, 10523265, 16141171, 56924),
    (403809289, 849839882, 304226562, 918367400, 134754959, 235584771, 753176364, 585109639, 550801639, 39983725, 5157, 0, 0, 0, 0, 0, 12069401, 8272911, 22228),
    (714083017, 825230434, 11324449, 44043912, 104506132, 926941188, 695217184, 112235029, 860886028, 46145079, 594106405, 39859303, 15840262, 14727215, 0, 0, 3711273, 7719744, 61398),
    (210806794, 438543746, 168953611, 272380779, 176992392, 687149411, 134517261, 168410925, 552122437, 41098533, 6182, 0, 0, 0, 0, 0, 13308570, 1037368, 26462),
    (3844810, 104616585, 2937513, 827327586, 34614276, 38590088, 5873707, 79730198, 114087936, 561001504, 114333702, 40909367, 15775815, 47, 0, 0, 4270394, 6342027, 65149),
    (211856395, 473706666, 507293833, 177475714, 135498509, 919766308, 274217096, 308066408, 134224463, 375423535, 39943, 0, 0, 0, 0, 0, 2702507, 6196500, 30223),
    (716247691, 682447908, 6083587, 38899370, 680538902, 929083394, 103326726, 1596454, 863024141, 7354401, 108569096, 100728878, 48143, 0, 0, 0, 12925515, 8508969, 61671),
    (145862668, 180106628, 145601956, 178526030, 308131971, 552832137, 43124998, 308448047, 7374017, 106568, 33063, 0, 0, 0, 0, 0, 15389884, 6486325, 1921),
    (717297292, 682727190, 6296374, 830123044, 3224614, 48029322, 7907848, 847289443, 69739534, 566318, 1148943, 34651168, 0, 0, 0, 0, 14070876, 10389306, 7938),
    (146912269, 180754190, 146249518, 341971727, 172801195, 8595814, 137632810, 309339432, 43124963, 1048674, 295009, 0, 0, 0, 0, 0, 16473805, 3639908, 297),
    (829495949, 863083181, 813700748, 717263879, 82616359, 116009988, 38282240, 649102121, 547425295, 36813825, 2197034, 34, 0, 0, 0, 0, 8897901, 16451918, 8611),
    (821147662, 854988941, 147298477, 343020808, 173318316, 212870503, 45393028, 335712257, 302000417, 103852227, 2082, 0, 0, 0, 0, 0, 9203198, 1358197, 9120),
    (75119368, 108706600, 814750349, 40674304, 15827629, 683677194, 38845505, 849380908, 548409410, 649168996, 35843, 0, 0, 0, 0, 0, 14063592, 10601968, 15140),
    (276937743, 310779022, 345414830, 311629965, 174306561, 147062794, 369235233, 312644716, 11831362, 37949483, 3107, 0, 0, 0, 0, 0, 14253711, 10862614, 13490),
)


def split(x):
    high = x.astype(BF16)
    return high, (x - high.astype(F32)).astype(BF16)


def across_lanes(both, blocks):
    return [
        both[:, 2 * n * TOK : (2 * n + 1) * TOK] + both[:, (2 * n + 1) * TOK : 2 * (n + 1) * TOK]
        for n in range(blocks)
    ]


def attend(kv, slots, masks, first, q_ref, acc, top, total):
    keys, values = [], []
    for slot in slots:
        k_high, k_low = split(kv[slot, 0:TOK, :])
        keys += [jnp.concatenate([k_high, k_high], axis=1), jnp.concatenate([k_low, k_low], axis=1)]
        values.append(jnp.concatenate(split(kv[slot, KEY_ROWS:ROWS, :]), axis=1))
    keys, values = jnp.concatenate(keys, axis=0), jnp.concatenate(values, axis=0)
    both = lax.dot_general(
        q_ref[...], keys, (((1,), (1,)), ((), ())), preferred_element_type=F32
    )
    scores = [
        jnp.where(jnp.concatenate([mask] * HEADS, axis=0), score, MASKED)
        for mask, score in zip(masks, across_lanes(both, len(slots)))
    ]
    high = functools.reduce(jnp.maximum, scores)
    high = jnp.broadcast_to(jnp.max(high, axis=1, keepdims=True), high.shape)
    if not first:
        old = top[...]
        high = jnp.maximum(old, high)
        factor = jnp.exp2(old - high)
    top[...] = high
    weights = [jnp.exp2(score - high) for score in scores]
    added = functools.reduce(jnp.add, weights)
    w_high, w_low = zip(*[split(weight) for weight in weights])
    both = jnp.dot(jnp.concatenate(w_high, axis=1), values, preferred_element_type=F32)
    rest = jnp.dot(jnp.concatenate(w_low, axis=1), values[:, :TOK], preferred_element_type=F32)
    mixed = across_lanes(both, 1)[0] + rest
    total[...] = added if first else total[...] * factor + added
    acc[...] = mixed if first else acc[...] * factor + mixed


def kernel(
    planes, queries, keys, values, segment, out, kv, seg_raw, q_raw, q_ref, acc, top, total,
    load_sem, send_sem, recv_sem,
):
    inner, outer = lax.axis_index("inner"), lax.axis_index("outer")
    x, z = lax.div(inner, RING), lax.rem(inner, RING)
    plane, core = lax.div(outer, 2), lax.rem(outer, 2)
    up, down, across = lax.rem(z + 1, RING), lax.rem(z + RING - 1, RING), 1 - x
    ahead, behind = lax.rem(plane + 1, planes), lax.rem(plane + planes - 1, planes)
    far = planes // 2

    def at(to_plane, to_x, to_z, to_core):
        return {"inner": to_x * RING + to_z, "outer": to_plane * 2 + to_core}

    loads = [
        pltpu.make_async_copy(segment, seg_raw, load_sem.at[0]),
        pltpu.make_async_copy(keys, kv.at[OWN, pl.ds(0, TOK)], load_sem.at[1]),
        pltpu.make_async_copy(values, kv.at[OWN, pl.ds(KEY_ROWS, TOK)], load_sem.at[2]),
        pltpu.make_async_copy(queries, q_raw, load_sem.at[3]),
    ]
    for load in loads:
        load.start()

    barrier = pltpu.get_barrier_semaphore()

    def greet(device):
        pl.semaphore_signal(barrier, inc=1, device_id=device, device_id_type=MESH)

    for to_x, to_z in ((x, up), (x, down), (across, z)):
        for to_core in (0, 1):
            greet(at(plane, to_x, to_z, to_core))
    greet(at(plane, x, z, 1 - core))

    @pl.when(core == 0)
    def _():
        greet(at(behind, x, z, 0))
        greet(at(behind, x, z, 1))

    @pl.when((core == 0) & (x == 0))
    def _():
        greet(at(behind, 1, z, 1))

    def lookup(options, n, each, width):
        word, rest = lax.div(n, each), lax.rem(n, each)
        packed = options[0]
        for k in range(1, len(options)):
            packed = jnp.where(word == k, options[k], packed)
        field = lax.rem(packed, 1 << width)
        for k in range(1, each):
            field = jnp.where(
                rest == k, lax.rem(lax.div(packed, 1 << (width * k)), 1 << width), field
            )
        return field

    def event_of(n):
        return lookup(words[:16], n, 3, 10)

    def slot_of(n):
        return lookup(words[16:], n, 6, 4)

    def bit(event, place):
        return lax.rem(lax.div(event, 1 << place), 2) == 1

    def piece(held, slot, part, device, way):
        first, count = PARTS[part]
        return pltpu.make_async_remote_copy(
            src_ref=kv.at[held, pl.ds(first, count)],
            dst_ref=kv.at[slot, pl.ds(first, count)],
            send_sem=send_sem.at[way, held, part],
            recv_sem=recv_sem.at[slot, part],
            device_id=device,
            device_id_type=MESH,
        )


    def absent(slot):
        kept = (lax.div(slot, RING) == x) & (lax.rem(slot, RING) < z)
        same = lax.div(slot, RING) == x
        return (plane == 0) & (core == 0) & (slot < PASSING) & ~kept & (same | (x == 0))

    def straight(to_x, hops):
        low = jnp.where(to_x == 0, 4, 2)
        return (hops >= low) & (hops <= low + 2)

    def direct(index):
        return (plane != planes - 1) & ((plane != far - 1) | straight(x, index - z))

    def onward(event, part, act):
        held = lax.rem(event, 32)
        index, passing = lax.rem(held, RING), held >= PASSING
        crossed = (held < PASSING) & (lax.div(held, RING) != x)
        is_o = passing | (~crossed & (core == 1) & (index < z))
        here = x * RING + index
        there = ~absent(held)
        for way, to_z in ((0, up), (1, down)):
            below = index < to_z
            to_core = jnp.where(below, jnp.where(is_o, 1, 0), jnp.where(is_o, across, 1))
            to_core = jnp.where(crossed, core, to_core)
            to_slot = jnp.where(is_o, jnp.where(below, here, PASSING + index), held)

            @pl.when(bit(event, 7 + way) & there)
            def _():
                act(piece(held, to_slot, part, at(plane, x, to_z, to_core), way))

        @pl.when(bit(event, 9) & ~(is_o & ~direct(index)))
        def _():
            aside = {
                "inner": jnp.where(is_o, inner, across * RING + z),
                "outer": jnp.where(is_o, ahead * 2, plane * 2 + x),
            }
            act(piece(held, here, part, aside, 2))

        from_near = (plane == far - 1) & (x == 1) & (core == 1)
        from_far = (plane == far) & (x == 0) & (core == 0)
        to_x = jnp.where(from_near, 0, 1)

        @pl.when(crossed & (index >= z) & (from_near | from_far) & ~straight(to_x, index - z))
        def _():
            act(piece(held, held, part, at(far, to_x, z, 0), 2))

    def own_onward(part, act):
        for way, to_z in ((0, up), (1, down)):
            hops = lax.rem(to_z - z + RING, RING)
            below = z < to_z
            to_core = jnp.where(below, core, jnp.where(core == 1, across, 1))
            to_slot = jnp.where((core == 1) & ~below, PASSING + z, inner)
            act(piece(OWN, to_slot, part, at(plane, x, to_z, to_core), way))

        @pl.when(core == 0)
        def _():
            act(piece(OWN, inner, part, at(plane, across, z, x), 2))
            act(piece(OWN, inner, part, at(plane, x, z, 1), 3))

        @pl.when((core == 1) & direct(z))
        def _():
            act(piece(OWN, inner, part, at(ahead, x, z, 0), 3))

        @pl.when((core == 1) & ((x == 0) | (plane != planes - 1)))
        def _():
            crossing = {
                "inner": across * RING + z,
                "outer": jnp.where(x == 0, plane * 2 + 1, ahead * 2),
            }
            act(piece(OWN, inner, part, crossing, 2))

    def start(copy):
        copy.start()

    def finish(copy):
        copy.wait_send()

    loads[0].wait()
    own_seg = seg_raw[...].astype(F32)
    kv[OWN, TOK:KEY_ROWS, :] = jnp.broadcast_to(own_seg, (8, TOK))
    pl.semaphore_wait(barrier, 8 + core * x)
    for part in (0, 1):
        loads[1 + part].wait()
        own_onward(part, start)

    place = inner * 2 + core + jnp.where(plane == far, 2 * SLOTS, 0)
    words = [jnp.int32(0)] * 19
    for row, packed in enumerate(PLAN):
        words = [jnp.where(place == row, jnp.int32(p), w) for p, w in zip(packed, words)]

    lead = own_seg[:, 0:1]
    pieces = 2 * (SLOTS + jnp.where(core == across, RING - 1 - z, 0))

    row = lax.broadcasted_iota(jnp.int32, (TOK, TOK), 0)
    col = lax.broadcasted_iota(jnp.int32, (TOK, TOK), 1)
    seg_row = jnp.broadcast_to(own_seg, (TOK, TOK))
    seg_col = seg_row.T

    def alone():
        scale = math.log2(math.e) / math.sqrt(TOK)
        for head in range(HEADS):
            rows = slice(head * TOK, (head + 1) * TOK)
            q_high, q_low = split(q_raw[:, rows] * scale)
            q_ref[rows, 0:TOK] = q_high
            q_ref[rows, TOK : 2 * TOK] = q_low

        attend(kv, [OWN], [(seg_col == seg_row) & (col <= row)], True, q_ref, acc, top, total)

    def pair(n):
        slots = [slot_of(2 * n), slot_of(2 * n + 1)]
        masks = []
        for slot in slots:
            seg = kv[slot, TOK : TOK + 1, :]
            shared = jnp.sum(jnp.where(seg == lead, 1.0, 0.0), axis=1, keepdims=True)
            masks.append((seg_col == lead) & (col.astype(F32) >= TOK - shared))
        attend(kv, slots, masks, False, q_ref, acc, top, total)

    def each_part(event, do):
        for part in (0, 1):

            @pl.when(bit(event, 5) == (part == 1))
            def _():
                do(part)

    def turn(done):
        @pl.when(done == 0)
        def _():
            alone()

        @pl.when(done > 0)
        def _():
            pair(done - 1)

    def step(n, done):
        event = event_of(n)

        def receive(part):
            slot = lax.rem(event, 32)
            first, count = PARTS[part]

            @pl.when(absent(slot))
            def _():
                kv[slot, first : first + count, :] = jnp.zeros((count, TOK), F32)
                if part == 0:
                    kv[slot, TOK:KEY_ROWS, :] = jnp.full((8, TOK), -1.0, F32)

            @pl.when(~absent(slot))
            def _():
                piece(slot, slot, part, at(plane, x, up, core), 0).wait_recv()
                onward(event, part, start)

        each_part(event, receive)
        now = bit(event, 6)

        @pl.when(now)
        def _():
            turn(done)

        @pl.when(n >= LAG)
        def _():
            drain(n - LAG, 0)

        return done + jnp.where(now, 1, 0)

    def drain(n, carry):
        event = event_of(n)

        crosses = (plane == far - 1) | (plane == far)

        @pl.when((event >= 1 << 7) | crosses)
        def _():
            each_part(event, lambda part: onward(event, part, finish))

        return carry

    loads[3].wait()
    done = lax.fori_loop(0, pieces, step, jnp.int32(0))

    def rest(n, carry):
        turn(n)
        return carry

    lax.fori_loop(done, SLOTS // 2 + 1, rest, 0)

    for head in range(HEADS):
        rows = slice(head * TOK, (head + 1) * TOK)
        out[:, rows] = acc[rows, :] / jnp.sum(total[rows, :], axis=1, keepdims=True)

    lax.fori_loop(pieces - LAG, pieces, drain, 0)
    for part in (0, 1):
        own_onward(part, finish)


def body(queries, keys, values, segment):
    planes = lax.axis_size("outer") // 2
    rows = HEADS * TOK
    return pl.pallas_call(
        functools.partial(kernel, planes),
        name="gather_and_attend",
        out_shape=pltpu.VMEM(queries.shape, F32),
        in_specs=[pl.BlockSpec(memory_space=pltpu.HBM)] * 4,
        out_specs=pl.BlockSpec(memory_space=pltpu.VMEM),
        scratch_shapes=[
            pltpu.VMEM((OWN + 1, ROWS, TOK), F32),
            pltpu.VMEM((1, TOK), jnp.int32),
            pltpu.VMEM((TOK, rows), F32),
            pltpu.VMEM((rows, 2 * TOK), BF16),
            pltpu.VMEM((rows, TOK), F32),
            pltpu.VMEM((rows, TOK), F32),
            pltpu.VMEM((rows, TOK), F32),
            pltpu.SemaphoreType.DMA((4,)),
            pltpu.SemaphoreType.DMA((4, OWN + 1, 2)),
            pltpu.SemaphoreType.DMA((OWN, 2)),
        ],
        compiler_params=pltpu.CompilerParams(
            collective_id=0, has_side_effects=True, vmem_limit_bytes=60 << 20
        ),
    )(queries, keys, values, segment.reshape(1, TOK))


def solution(mesh):
    return jax.shard_map(
        body,
        mesh=mesh,
        in_specs=(
            P(("outer", "inner"), None),
            P(("outer", "inner"), None),
            P(("outer", "inner"), None),
            P(("outer", "inner")),
        ),
        out_specs=P(("outer", "inner"), None),
        check_vma=False,
    )
```

time: 42.4 us -> 40.4 us (0.953); the launches traced: 42.3 us -> 39.7 us
  Pallas kernels: 41.5 us -> 38.9 us
    pallas_call x1, Pallas kernels: 41.5 us -> 38.9 us  [body(): pl.pallas_call(functools.partial(kernel, planes), name='gather_and_attend...]
where the time goes in v3:
time: 40.4 us; the launch traced here: 39.7 us
  Pallas kernels  38.9 us (96%)
  local copies, waits for them, and re-layouts  0.8 us (2%)
    pallas_call x1, Pallas kernels, body(): pl.pallas_call(functools.partial(kernel, planes), name='gather_and_attend...  38.9 us

profile of v3, /device:TPU:6, one launch (start us, length us, event | category | flops | bytes accessed | tf_op | source)
XLA Modules:
  0.0 39.7 jit_solution(10598508971575171255)
XLA Ops:
  0.0 38.9 %gather_and_attend.1 = f32[128,1024]{1,0:T(8,128)S(1)} custom-call(f32[128,1024]{1,0:T(8,128)} %queries.1, f32[128,128]{1,0:T(8,128)} %keys.1, f32[128,128]{1,0:T(8,128)} %values.1, s32[1,128]{1,0:T(1,128)} %bitcast.1), custom_call_target="tpu_custom_call" | custom-call | tf_op jit(solution)/shard_map/gather_and_attend/pallas_call | solution.py:408
  38.9 0.8 %copy.6 = f32[128,1024]{1,0:T(8,128)} copy(f32[128,1024]{1,0:T(8,128)S(1)} %gather_and_attend.1) | data formatting | bytes 1048576

commit v4 on v3

--- a/solution.py
+++ b/solution.py
@@ -19,7 +19,7 @@
 OWN = SLOTS + RING
 KEY_ROWS = TOK + 8
 ROWS = KEY_ROWS + TOK
-PARTS = ((0, KEY_ROWS), (KEY_ROWS, TOK))
+PARTS = ((0, TOK), (TOK, ROWS - TOK))
 UP_HOPS = (4, 3)
 LAG = 12
 MASKED = -1e30
@@ -200,8 +200,9 @@
 
     def piece(held, slot, part, device, way):
         first, count = PARTS[part]
+        here = keys if held is OWN and part == 0 else kv.at[held, pl.ds(first, count)]
         return pltpu.make_async_remote_copy(
-            src_ref=kv.at[held, pl.ds(first, count)],
+            src_ref=here,
             dst_ref=kv.at[slot, pl.ds(first, count)],
             send_sem=send_sem.at[way, held, part],
             recv_sem=recv_sem.at[slot, part],
@@ -286,18 +287,20 @@
     def finish(copy):
         copy.wait_send()
 
-    loads[0].wait()
-    own_seg = seg_raw[...].astype(F32)
-    kv[OWN, TOK:KEY_ROWS, :] = jnp.broadcast_to(own_seg, (8, TOK))
     pl.semaphore_wait(barrier, 8 + core * x)
-    for part in (0, 1):
-        loads[1 + part].wait()
-        own_onward(part, start)
+    own_onward(0, start)
 
     place = inner * 2 + core + jnp.where(plane == far, 2 * SLOTS, 0)
     words = [jnp.int32(0)] * 19
     for row, packed in enumerate(PLAN):
         words = [jnp.where(place == row, jnp.int32(p), w) for p, w in zip(packed, words)]
+
+    loads[0].wait()
+    own_seg = seg_raw[...].astype(F32)
+    kv[OWN, TOK:KEY_ROWS, :] = jnp.broadcast_to(own_seg, (8, TOK))
+    loads[2].wait()
+    own_onward(1, start)
+    loads[1].wait()
 
     lead = own_seg[:, 0:1]
     pieces = 2 * (SLOTS + jnp.where(core == across, RING - 1 - z, 0))
@@ -352,7 +355,7 @@
             @pl.when(absent(slot))
             def _():
                 kv[slot, first : first + count, :] = jnp.zeros((count, TOK), F32)
-                if part == 0:
+                if part == 1:
                     kv[slot, TOK:KEY_ROWS, :] = jnp.full((8, TOK), -1.0, F32)
 
             @pl.when(~absent(slot))

time: 40.4 us -> 40.6 us (level)
  Pallas kernels: 38.9 us -> 39.5 us
    pallas_call x1, Pallas kernels: 38.9 us -> 39.5 us  [body(): pl.pallas_call(functools.partial(kernel, planes), name='gather_and_attend...]
where the time goes in v4:
time: 40.6 us; the launch traced here: 40.3 us
  Pallas kernels  39.5 us (97%)
  local copies, waits for them, and re-layouts  0.8 us (2%)
    pallas_call x1, Pallas kernels, body(): pl.pallas_call(functools.partial(kernel, planes), name='gather_and_attend...  39.5 us

profile of v4, /device:TPU:6, one launch (start us, length us, event | category | flops | bytes accessed | tf_op | source)
XLA Modules:
  0.0 40.3 jit_solution(9361163980294877507)
XLA Ops:
  0.0 39.5 %gather_and_attend.1 = f32[128,1024]{1,0:T(8,128)S(1)} custom-call(f32[128,1024]{1,0:T(8,128)} %queries.1, f32[128,128]{1,0:T(8,128)} %keys.1, f32[128,128]{1,0:T(8,128)} %values.1, s32[1,128]{1,0:T(1,128)} %bitcast.1), custom_call_target="tpu_custom_call" | custom-call | tf_op jit(solution)/shard_map/gather_and_attend/pallas_call | solution.py:411
  39.5 0.8 %copy.6 = f32[128,1024]{1,0:T(8,128)} copy(f32[128,1024]{1,0:T(8,128)S(1)} %gather_and_attend.1) | data formatting | bytes 1048576
